TPU v7x, 32 devices: a whole 2x2x4 slice. The times are simulated.
32 devices in a mesh: seq: 8 (over z, y), tower: 4 (over x, core).
Axes of the slice: x: 2, y: 2, z: 4, core: 2. Of those that a mesh axis runs over, the one named last changes fastest.
Arguments:
- inputs: bfloat16 [4, 1024, 4096], P('tower', 'seq'), may hold values from -21 to 21
- modality: int32 [4, 1024], P('tower', 'seq'), may hold values from 0 to 1, as said below
- segment: int32 [4, 1024], P('tower', 'seq'), may hold values from 0 to 7, never falling along the last dimension, each value on 1 to 512 neighbouring positions
- w_qkv: bfloat16 [2, 16, 4096, 384], P(None, 'seq', 'tower'), may hold values from -0.09375 to 0.09375
- w_out: bfloat16 [2, 16, 128, 4096], P(None, 'seq', None, 'tower'), may hold values from -0.5 to 0.5
Outputs:
- attended: bfloat16 [4, 1024, 4096], P('tower', 'seq')
Inputs may be any that keep to these rules, and one draw needn't show every extreme that they name: `modality`: image positions come in contiguous runs. `segment`: within each packed sequence the document number never falls; every document holds 1 to 512 positions and one holds exactly 512.
All inputs are finite; a program needn't handle non-finite values.
Results may differ from a plain program's by a relative error of at most 0.012.
The roundings to bfloat16 on the way count: a program that leaves them out, or rounds other values in their place, can miss the bound.
Values may be sent and summed in bfloat16 or wider, within the bound.
A program may use at most 128 MiB of HBM per device.

v0:
```python
import math

import jax
import jax.numpy as jnp
from jax import lax
from jax.sharding import PartitionSpec as P


def key_scores(q_block, keys_tile):
    return lax.dot_general(
        q_block, keys_tile, (((1,), (1,)), ((), ())), preferred_element_type=jnp.float32
    )


def dense_attend(queries, keys_all, values_all, doc_ids, score_scale):
    length = queries.shape[0]
    head_size = queries.shape[1]
    block_rows = min(512, length)
    positions = jnp.arange(length, dtype=jnp.int32)

    def one_block(block_idx):
        first_row = block_idx * block_rows
        q_block = lax.dynamic_slice_in_dim(queries, first_row, block_rows, 0)
        q_docs = lax.dynamic_slice_in_dim(doc_ids, first_row, block_rows, 0)
        q_pos = first_row + jnp.arange(block_rows, dtype=jnp.int32)
        scores = key_scores(q_block, keys_all) * score_scale
        allowed = (q_docs[:, None] == doc_ids[None, :]) & (positions[None, :] <= q_pos[:, None])
        scores = jnp.where(allowed, scores, -jnp.inf)
        row_top = jnp.max(scores, axis=1, keepdims=True)
        expon = jnp.exp(scores - row_top)
        probs = (expon / jnp.sum(expon, axis=1, keepdims=True)).astype(jnp.bfloat16)
        return jnp.dot(probs, values_all, preferred_element_type=jnp.float32).astype(jnp.bfloat16)

    outputs = lax.map(one_block, jnp.arange(length // block_rows, dtype=jnp.int32))
    return outputs.reshape(length, head_size)


def qkv_product(row_block, weight):
    return jnp.einsum("rd,hde->rhe", row_block, weight, preferred_element_type=jnp.float32)


def out_product(row_block, weight):
    return jnp.einsum("rhc,hcd->rd", row_block, weight, preferred_element_type=jnp.float32)


def local(inputs, modality, segment, w_qkv, w_out):
    tok_rows = inputs.shape[1]
    seq_devices = lax.axis_size("seq")
    length = tok_rows * seq_devices
    head_group = w_qkv.shape[1]
    head_size = w_out.shape[2]
    score_scale = 1.0 / math.sqrt(head_size)
    weights = lax.all_gather(w_qkv, "tower", axis=2, tiled=True)
    start_carry = (
        jnp.zeros((length, head_group, 3 * head_size), jnp.float32),
        jnp.zeros((length,), jnp.int32),
        jnp.zeros((length,), jnp.int32),
    )
    first_row = jnp.int32(0)
    row_piece = lax.all_gather(inputs, "seq", axis=1, tiled=True)
    modal_piece = lax.all_gather(modality, "seq", axis=1, tiled=True)
    doc_piece = lax.all_gather(segment, "seq", axis=1, tiled=True)
    text_part = qkv_product(row_piece[0], weights[0])
    image_part = qkv_product(row_piece[0], weights[1])
    selected = jnp.where(modal_piece[0][:, None, None] == 1, image_part, text_part)
    projected = selected
    modal_all = lax.dynamic_update_slice_in_dim(start_carry[1], modal_piece[0], first_row, 0)
    doc_all = lax.dynamic_update_slice_in_dim(start_carry[2], doc_piece[0], first_row, 0)
    projected = projected.astype(jnp.bfloat16)
    head_list = []
    for head_idx in range(head_group):
        queries = projected[:, head_idx, :head_size]
        keys_all = projected[:, head_idx, head_size : 2 * head_size]
        values_all = projected[:, head_idx, 2 * head_size :]
        head_list.append(dense_attend(queries, keys_all, values_all, doc_all, score_scale))
    head_out = jnp.stack(head_list, axis=0)
    columns = lax.all_gather(w_out, "tower", axis=3, tiled=True)
    out_rows = head_out
    out_rows = jnp.transpose(out_rows, (1, 0, 2))
    text_out = out_product(out_rows, columns[0])
    image_out = out_product(out_rows, columns[1])
    summed = lax.psum_scatter(
        jnp.where(modal_all[:, None] == 1, image_out, text_out).astype(jnp.bfloat16),
        "seq",
        scatter_dimension=0,
        tiled=True,
    )
    return summed[None]


def solution(mesh):
    return jax.shard_map(
        local,
        mesh=mesh,
        in_specs=(
            P("tower", "seq", None),
            P("tower", "seq"),
            P("tower", "seq"),
            P(None, "seq", "tower", None),
            P(None, "seq", None, "tower"),
        ),
        out_specs=P("tower", "seq", None),
        check_vma=False,
    )
```

profile of v0, /device:TPU:0, one launch (start us, length us, event | category | flops | bytes accessed | tf_op | source)
XLA Modules:
  0.0 420.4 jit_solution(945094070977211416)
XLA Ops:
  6.5 0.7 all-gather.4.cloned.1.call-update
  7.3 0.7 all-gather.6.cloned.1.call-update
  8.1 0.7 all-gather.8.cloned.1.call-update
  8.8 22.2 %all_gather.15 = s32[1,1024]{1,0:T(1,128)S(1)} all-gather(s32[1,128]{1,0:T(1,128)S(1)} %copy-done.1), channel_id=1, replica_groups=mesh['seq'=8,'tower'=4] {'seq'}, dimensions={1}, use_global_device_ids=true | all-gather | bytes 4608 | tf_op jit(solution)/shard_map/all_gather | solution.py:61
  31.1 16.3 %all_gather.16 = s32[1,1024]{1,0:T(1,128)S(1)} all-gather(s32[1,128]{1,0:T(1,128)S(1)} %copy-done.2), channel_id=1, replica_groups=mesh['seq'=8,'tower'=4] {'seq'}, dimensions={1}, use_global_device_ids=true | all-gather | bytes 4608 | tf_op jit(solution)/shard_map/all_gather | solution.py:62
  47.4 89.7 %all-gather.4.cloned.1.call-done = bf16[1,1024,4096]{2,1,0:T(8,128)(2,1)} async-done(((bf16[1,128,4096]{2,1,0:T(8,128)(2,1)}), bf16[1,1024,4096]{2,1,0:T(8,128)(2,1)}) %all-gather.4.cloned.1.call-update) | async-done | bytes 8388624 | tf_op jit(solution)/shard_map/all_gather | solution.py:60
  137.2 81.9 %all-gather.6.cloned.1.call-done = bf16[2,2,4096,384]{3,2,1,0:T(8,128)(2,1)} async-done(((bf16[2,2,1024,384]{3,2,1,0:T(8,128)(2,1)}), bf16[2,2,4096,384]{3,2,1,0:T(8,128)(2,1)}) %all-gather.6.cloned.1.call-update) | async-done | bytes 12582928 | tf_op jit(solution)/shard_map/all_gather | solution.py:53
  219.0 11.8 %fusion.17 = bf16[1024,2,384]{2,0,1:T(8,128)(2,1)S(1)} fusion(bf16[1,1024,4096]{2,1,0:T(8,128)(2,1)} %all-gather.4.cloned.1.call-done, bf16[2,2,4096,384]{3,2,1,0:T(8,128)(2,1)} %all-gather.6.cloned.1.call-done), kind=kOutput, calls=%fused_computation.28 | convolution fusion | flops 6442450944 | bytes 16252928 | tf_op jit(solution)/shard_map/rd,hde->rhe/dot_general | solution.py:39
  230.8 0.8 copy-done.4
  231.7 6.7 %select_convert_fusion = bf16[1024,2,384]{2,0,1:T(8,128)(2,1)S(1)} fusion(bf16[1024,2,384]{2,0,1:T(8,128)(2,1)S(1)} %fusion.17, bf16[2,2,4096,384]{3,2,1,0:T(8,128)(2,1)S(1)} %copy-done.3, bf16[1,1024,4096]{2,1,0:T(8,128)(2,1)S(1)} %copy-done.4, pred[1024]{0:T(1024)(128)(4,1)S(1)} %compare_reduce_fusion), kind=kOutput, calls=%fused_computation.34 | convolution fusion | flops 6443237376 | bytes 17826816 | tf_op jit(solution)/shard_map/rd,hde->rhe/dot_general | solution.py:39
  238.7 6.3 %while.22 = (s32[]{:T(128)}, bf16[2,512,128]{2,1,0:T(8,128)(2,1)S(1)}, s32[2]{0:T(128)S(1)}, s32[1024]{0:T(1024)S(1)}, s32[1,1024]{1,0:T(1,128)S(1)}, /*index=5*...) while((s32[]{:T(128)}, ...), condition=%wide.region_3.4_spmd.clone, body=%wide.region_0.3_spmd.clone.sunk | while | flops 274267648 | bytes 7102655 | solution.py:34
  240.0 0.7 fusion.44
  241.2 0.6 fusion.46
  243.1 0.7 fusion.44
  244.4 0.6 fusion.46
  245.1 6.3 %while.23 = (s32[]{:T(128)}, bf16[2,512,128]{2,1,0:T(8,128)(2,1)S(1)}, s32[2]{0:T(128)S(1)}, s32[1024]{0:T(1024)S(1)}, s32[1,1024]{1,0:T(1,128)S(1)}, /*index=5*...) while((s32[]{:T(128)}, ...), condition=%wide.region_7.8_spmd.clone, body=%wide.region_4.7_spmd.clone.sunk | while | flops 274267648 | bytes 7102655 | solution.py:34
  246.4 0.7 fusion.49
  247.6 0.6 fusion.51
  249.6 0.7 fusion.49
  250.8 0.6 fusion.51
  251.4 3.7 all-gather.8.cloned.1.call-done
  255.1 4.3 %fusion.21 = bf16[1024,4096,1]{1,0,2:T(8,128)(2,1)S(1)} fusion(bf16[2,2,128,4096]{3,2,1,0:T(8,128)(2,1)} %all-gather.8.cloned.1.call-done, bf16[1,1024,128]{2,1,0:T(8,128)(2,1)S(1)} %bitcast.84, bf16[1,1024,128]{2,1,0:T(8,128)(2,1)S(1)} %bitcast.86), kind=kOutput, calls=%fused_computation.37 | convolution fusion | flops 2147745792 | bytes 11010048 | tf_op jit(solution)/shard_map/rhc,hcd->rd/dot_general | solution.py:43
  259.4 4.8 %fusion.16 = bf16[1024,4096]{1,0:T(8,128)(2,1)} fusion(bf16[1024,4096,1]{1,0,2:T(8,128)(2,1)S(1)} %fusion.21, pred[1024]{0:T(1024)(128)(4,1)S(1)} %compare_reduce_fusion, bf16[2,2,128,4096]{3,2,1,0:T(8,128)(2,1)S(1)} %copy-done, bf16[1,1024,128]{2,1,0:T(8,128)(2,1)S(1)} %bitcast.85, bf16[1,1024,128]{2,1,0:T(8,128)(2,1)S(1)} %bitcast.87), kind=kOutput, calls=%fused_computation.27 | convolution fusion | flops 2151940096 | bytes 19399680 | tf_op jit(solution)/shard_map/rhc,hcd->rd/dot_general | solution.py:43
  264.3 149.6 %reduce-scatter.2.cloned.1.call-done = bf16[128,4096]{1,0:T(8,128)(2,1)} async-done(((bf16[1024,4096]{1,0:T(8,128)(2,1)}), bf16[128,4096]{1,0:T(8,128)(2,1)}) %reduce-scatter.2.cloned.1.call-update) | async-done | bytes 1048592 | tf_op jit(solution)/shard_map/reduce_scatter | solution.py:82
  (36 shorter events, 5.3 us)
Async XLA Ops:
  6.5 130.6 %all-gather.4.cloned.1.call-start = ((), (), s32[]{:S(2)}) async-start(), calls=%async_computation.1 | async-start | bytes 9437184 | tf_op jit(solution)/shard_map/all_gather | solution.py:60
  7.3 1.6 copy-start.1
  7.3 23.8 %copy-start.2 = (s32[1,128]{1,0:T(1,128)S(1)}, s32[1,128]{1,0:T(1,128)}, u32[]{:S(2)}) copy-start(s32[1,128]{1,0:T(1,128)} %param.11) | copy-start | bytes 1540
  7.3 211.8 %all-gather.6.cloned.1.call-start = ((), (), s32[]{:S(2)}) async-start(), calls=%async_computation.2 | async-start | bytes 15728640 | tf_op jit(solution)/shard_map/all_gather | solution.py:53
  8.0 247.1 %all-gather.8.cloned.1.call-start = ((), (), s32[]{:S(2)}) async-start(), calls=%async_computation.3 | async-start | bytes 5242880 | tf_op jit(solution)/shard_map/all_gather | solution.py:77
  8.8 405.1 %reduce-scatter.2.cloned.1.call-start = ((), (), s32[]{:S(2)}) async-start(), calls=%async_computation.4 | async-start | bytes 9437184 | tf_op jit(solution)/shard_map/reduce_scatter | solution.py:82
  219.0 11.8 %copy-start.3 = (bf16[2,2,4096,384]{3,2,1,0:T(8,128)(2,1)S(1)}, bf16[2,2,4096,384]{3,2,1,0:T(8,128)(2,1)}, u32[]{:S(2)}) copy-start(bf16[2,2,4096,384]{3,2,1,0:T(8,128)(2,1)} %all-gather.6.cloned.1.call-done) | copy-start | bytes 37748740
  219.0 12.6 %copy-start.4 = (bf16[1,1024,4096]{2,1,0:T(8,128)(2,1)S(1)}, bf16[1,1024,4096]{2,1,0:T(8,128)(2,1)}, u32[]{:S(2)}) copy-start(bf16[1,1024,4096]{2,1,0:T(8,128)(2,1)} %all-gather.4.cloned.1.call-done) | copy-start | bytes 25165828
  255.1 4.3 %copy-start = (bf16[2,2,128,4096]{3,2,1,0:T(8,128)(2,1)S(1)}, bf16[2,2,128,4096]{3,2,1,0:T(8,128)(2,1)}, u32[]{:S(2)}) copy-start(bf16[2,2,128,4096]{3,2,1,0:T(8,128)(2,1)} %all-gather.8.cloned.1.call-done) | copy-start | bytes 12582916
Sparse Core Ops, SparseCore 0:
  9.5 127.6 all-gather.3
  138.7 80.2 all-gather.5
  220.6 34.4 all-gather.7
  264.4 149.4 reduce-scatter.1
where the time goes:
time: 421 us; the launch traced here: 420 us
  waiting for transfers between devices  327 us (78%)
  blocking collectives  38.6 us (9%)
  matrix products  32.9 us (8%)
  between operations  13.3 us (3%)
    reduce_scatter x1, waiting for transfers between devices, local(): lax.psum_scatter(jnp.where(modal_all[:, None] == 1, image_out, text_out)....  150 us
    all_gather x1, waiting for transfers between devices, local(): row_piece = lax.all_gather(inputs, 'seq', axis=1, tiled=True)  89.7 us
    all_gather x1, waiting for transfers between devices, local(): weights = lax.all_gather(w_qkv, 'tower', axis=2, tiled=True)  81.9 us
    all_gather x1, blocking collectives, local(): modal_piece = lax.all_gather(modality, 'seq', axis=1, tiled=True)  22.2 us
    dot_general x2, matrix products, qkv_product(): jnp.einsum('rd,hde->rhe', row_block, weight, preferred_element_type=jnp.f...  18.4 us
    all_gather x1, blocking collectives, local(): doc_piece = lax.all_gather(segment, 'seq', axis=1, tiled=True)  16.3 us
    dot_general x2, matrix products, out_product(): jnp.einsum('rhc,hcd->rd', row_block, weight, preferred_element_type=jnp.f...  9.09 us
  transfers between devices with their start and end apart: 4, of which 4 were waited for; matrix products, arithmetic and copies ran while one was open for 7% of the time, Pallas kernels for 0%

commit v1 on v0

--- a/solution.py
+++ b/solution.py
@@ -3,6 +3,8 @@
 import jax
 import jax.numpy as jnp
 from jax import lax
+from jax.experimental import pallas as pl
+from jax.experimental.pallas import tpu as pltpu
 from jax.sharding import PartitionSpec as P
 
 
@@ -88,9 +90,342 @@
     return summed[None]
 
 
+MESH = pl.DeviceIdType.MESH
+
+
+def coords():
+    s, t = lax.axis_index("seq"), lax.axis_index("tower")
+    return s, t, s // 2, s % 2, t // 2, t % 2
+
+
+def enter(peers):
+    barrier = pltpu.get_barrier_semaphore()
+    for peer in peers:
+        pl.semaphore_signal(barrier, inc=1, device_id=peer, device_id_type=MESH)
+    pl.semaphore_wait(barrier, len(peers))
+
+
+def remote(src, dst, send, recv, peer):
+    return pltpu.make_async_remote_copy(
+        src_ref=src, dst_ref=dst, send_sem=send, recv_sem=recv,
+        device_id=peer, device_id_type=MESH,
+    )
+
+
+def gather_kernel(
+    tok, meta, w, tok_all, meta_all, w_all,
+    local_sem, up_send, dn_send, z_recv, y_send, y_recv,
+    w_send, w_recv, m_send, m_recv, mt_send, mt_recv,
+):
+    s, t, z, y, x, c = coords()
+    rows = tok.shape[0]
+    depth = w.shape[2]
+    x_peer = (s, (1 - x) * 2 + c)
+    core_peer = (s, x * 2 + (1 - c))
+    diagonal = (s, (1 - x) * 2 + (1 - c))
+    y_peer = (z * 2 + (1 - y), t)
+    seq_peers = [(lax.rem(s + k, 8), t) for k in range(1, 8)]
+    enter(seq_peers + [x_peer, core_peer, diagonal])
+
+    def tok_at(block):
+        return tok_all.at[pl.ds(pl.multiple_of(block * rows, rows), rows)]
+
+    def w_at(owner, m, h):
+        return w_all.at[m, h, pl.ds(pl.multiple_of(owner * depth, depth), depth)]
+
+    chunks = [(m, h) for m in range(w.shape[0]) for h in range(w.shape[1])]
+
+    def up(o, src):
+        return remote(src, tok_at(o * 2 + y), up_send.at[o], z_recv.at[o], (s + 2, t))
+
+    def down(o, src):
+        return remote(src, tok_at(o * 2 + y), dn_send.at[o], z_recv.at[o], (s - 2, t))
+
+    def across(o, src):
+        return remote(src, tok_at(o * 2 + y), y_send.at[o], y_recv.at[o], y_peer)
+
+    def w_copy(kind, k, src, owner, peer):
+        m, h = chunks[k]
+        return remote(src, w_at(owner, m, h), w_send.at[kind, k], w_recv.at[kind, k], peer)
+
+    @pl.when(z < 3)
+    def _():
+        up(z, tok).start()
+
+    @pl.when(z > 0)
+    def _():
+        down(z, tok).start()
+
+    across(z, tok).start()
+    for k, (m, h) in enumerate(chunks):
+        w_copy(0, k, w.at[m, h], t, x_peer).start()
+    meta_copies = [
+        remote(meta, meta_all.at[t, s], m_send.at[k], m_recv.at[k], peer)
+        for k, peer in enumerate(seq_peers)
+    ]
+    for copy in meta_copies:
+        copy.start()
+    for k, (m, h) in enumerate(chunks):
+        w_copy(1, k, w.at[m, h], t, core_peer).start()
+    own = [
+        pltpu.make_async_copy(tok, tok_at(s), local_sem.at[0]),
+        pltpu.make_async_copy(meta, meta_all.at[t, s], local_sem.at[1]),
+        pltpu.make_async_copy(
+            w, w_all.at[:, :, pl.ds(pl.multiple_of(t * depth, depth), depth)], local_sem.at[2]
+        ),
+    ]
+    for copy in own:
+        copy.start()
+
+    def pass_weights(k):
+        m, h = chunks[k]
+        w_copy(0, k, w.at[m, h], t, x_peer).wait_recv()
+        w_copy(2, k, w_at(x_peer[1], m, h), x_peer[1], core_peer).start()
+
+    n_chunks = len(chunks)
+    for d in range(1, 4):
+        if d - 1 < n_chunks:
+            pass_weights(d - 1)
+        low, high = z - d, z + d
+
+        @pl.when(low >= 0)
+        def _():
+            up(low, tok_at(low * 2 + y)).wait_recv()
+
+            @pl.when(z < 3)
+            def _():
+                up(low, tok_at(low * 2 + y)).start()
+
+            across(low, tok_at(low * 2 + y)).start()
+
+        @pl.when(high <= 3)
+        def _():
+            down(high, tok_at(high * 2 + y)).wait_recv()
+
+            @pl.when(z > 0)
+            def _():
+                down(high, tok_at(high * 2 + y)).start()
+
+            across(high, tok_at(high * 2 + y)).start()
+
+    for k in range(3, n_chunks):
+        pass_weights(k)
+    for copy in own:
+        copy.wait()
+    for copy in meta_copies:
+        copy.wait()
+    tower_meta = [
+        remote(meta_all.at[t], meta_all.at[t], mt_send.at[k], mt_recv.at[k], peer)
+        for k, peer in enumerate((x_peer, core_peer, diagonal))
+    ]
+    for copy in tower_meta:
+        copy.start()
+    for o in range(4):
+        across(o, tok).wait()
+
+        @pl.when((z < 3) & (o <= z))
+        def _():
+            up(o, tok).wait_send()
+
+        @pl.when((z > 0) & (o >= z))
+        def _():
+            down(o, tok).wait_send()
+
+    for k, (m, h) in enumerate(chunks):
+        w_copy(0, k, w.at[m, h], t, x_peer).wait_send()
+        w_copy(1, k, w.at[m, h], t, core_peer).wait()
+        w_copy(2, k, w.at[m, h], t, core_peer).wait()
+    for copy in tower_meta:
+        copy.wait()
+
+
+def gather_all(tok, meta, w):
+    dma = pltpu.SemaphoreType.DMA
+    hbm = pl.BlockSpec(memory_space=pl.ANY)
+    heads = w.shape[1]
+    return pl.pallas_call(
+        gather_kernel,
+        out_shape=(
+            jax.ShapeDtypeStruct((tok.shape[0] * 8, tok.shape[1]), tok.dtype),
+            jax.ShapeDtypeStruct((4, 8) + meta.shape, meta.dtype),
+            jax.ShapeDtypeStruct((2, heads, w.shape[2] * 4, w.shape[3]), w.dtype),
+        ),
+        in_specs=[hbm] * 3,
+        out_specs=(hbm, hbm, hbm),
+        scratch_shapes=[
+            dma((3,)), dma((4,)), dma((4,)), dma((4,)), dma((4,)), dma((4,)),
+            dma((3, 2 * heads)), dma((3, 2 * heads)), dma((7,)), dma((7,)), dma((3,)), dma((3,)),
+        ],
+        compiler_params=pltpu.CompilerParams(collective_id=0, has_side_effects=True),
+        cost_estimate=pl.CostEstimate(flops=0, bytes_accessed=42 << 20, transcendentals=0),
+    )(tok, meta, w)
+
+
+def out_kernel(
+    ho, mask, w, out, got, lhs, keep, sent, arrived, ready,
+    z_send, z_recv, g_send, g_recv, y_send, y_recv, o_send, o_recv,
+):
+    s, t, z, y, x, c = coords()
+    rows = ho.shape[0] // 4
+    half = rows // 2
+    width = ho.shape[1]
+    cols = w.shape[2]
+    order = [t, x * 2 + (1 - c), (1 - x) * 2 + c, (1 - x) * 2 + (1 - c)]
+    x_peer, core_peer = (s, order[2]), (s, order[1])
+    y_peer = (z * 2 + (1 - y), t)
+    z_peers = [(lax.rem(s + 2 * k, 8), t) for k in range(1, 4)]
+    enter(z_peers + [(s, o) for o in order[1:]] + [y_peer])
+
+    def rows_of(block, n):
+        return pl.ds(pl.multiple_of(block * n, n), n)
+
+    z_copies = [
+        remote(
+            ho.at[rows_of(lax.rem(z + k, 4), rows)], got.at[t, z],
+            z_send.at[k - 1], z_recv.at[k - 1], z_peers[k - 1],
+        )
+        for k in range(1, 4)
+    ]
+    for copy in z_copies:
+        copy.start()
+    got[t, z] = ho[rows_of(z, rows)]
+    for copy in z_copies:
+        copy.wait_recv()
+    g_copies = [
+        remote(got.at[t], got.at[t], g_send.at[0], g_recv.at[0], x_peer),
+        remote(got.at[t], got.at[t], g_send.at[1], g_recv.at[1], core_peer),
+        remote(got.at[order[2]], got.at[order[2]], g_send.at[2], g_recv.at[2], core_peer),
+    ]
+    g_copies[0].start()
+    g_copies[1].start()
+
+    def project(j):
+        owner = order[j]
+        for g in range(4):
+            block = got[owner, g]
+            m = mask[owner]
+            for h in range(width // 128):
+                part = block[:, h * 128:(h + 1) * 128]
+                image = part * m
+                lhs[g, :, h * 128:(h + 1) * 128] = part - image
+                lhs[g, :, width + h * 128:width + (h + 1) * 128] = image
+
+        @pl.loop(0, cols // 256)
+        def _(tile):
+            at = rows_of(tile, 256)
+            for away in range(2):
+                side = (1 - y) if away else y
+                total = None
+                for g in range(4):
+                    part = jnp.dot(
+                        lhs[g, rows_of(side, half), :], w[g, :, at],
+                        preferred_element_type=jnp.float32,
+                    ).astype(jnp.bfloat16).astype(jnp.float32)
+                    total = part if total is None else total + part
+                if away:
+                    sent[j, :, at] = total.astype(jnp.bfloat16)
+                else:
+                    keep[j, :, at] = total
+
+    y_copies = [
+        remote(sent.at[j], arrived.at[j], y_send.at[j], y_recv.at[j], y_peer) for j in range(4)
+    ]
+    my_cols = rows_of(t, cols)
+    o_copies = [
+        remote(ready.at[j], out.at[:, my_cols], o_send.at[j - 1], o_recv.at[j - 1], (s, order[j]))
+        for j in range(1, 4)
+    ]
+
+    def finish(j):
+        y_copies[j].wait_recv()
+        total = (keep[j] + arrived[j].astype(jnp.float32)).astype(jnp.bfloat16)
+        if j == 0:
+            out[:, my_cols] = total
+        else:
+            ready[j] = total
+            o_copies[j - 1].start()
+
+    project(0)
+    y_copies[0].start()
+    g_copies[1].wait_recv()
+    project(1)
+    y_copies[1].start()
+    g_copies[0].wait_recv()
+    g_copies[2].start()
+    project(2)
+    y_copies[2].start()
+    finish(1)
+    g_copies[2].wait_recv()
+    project(3)
+    y_copies[3].start()
+    finish(0)
+    finish(2)
+    finish(3)
+    for copy in z_copies + g_copies + y_copies:
+        copy.wait_send()
+    for copy in o_copies:
+        copy.wait()
+
+
+def out_project(ho, mask, w):
+    dma = pltpu.SemaphoreType.DMA
+    vmem = pl.BlockSpec(memory_space=pltpu.VMEM)
+    rows, cols, width = ho.shape[0] // 4, w.shape[2], ho.shape[1]
+    return pl.pallas_call(
+        out_kernel,
+        out_shape=jax.ShapeDtypeStruct((rows // 2, cols * 4), jnp.bfloat16),
+        in_specs=[vmem] * 3,
+        out_specs=vmem,
+        scratch_shapes=[
+            pltpu.VMEM((4, 4, rows, width), jnp.bfloat16),
+            pltpu.VMEM((4, rows, 2 * width), jnp.bfloat16),
+            pltpu.VMEM((4, rows // 2, cols), jnp.float32),
+            pltpu.VMEM((4, rows // 2, cols), jnp.bfloat16),
+            pltpu.VMEM((4, rows // 2, cols), jnp.bfloat16),
+            pltpu.VMEM((4, rows // 2, cols), jnp.bfloat16),
+            dma((3,)), dma((3,)), dma((3,)), dma((3,)), dma((4,)), dma((4,)), dma((3,)), dma((3,)),
+        ],
+        compiler_params=pltpu.CompilerParams(
+            collective_id=1, has_side_effects=True, vmem_limit_bytes=40 << 20
+        ),
+        cost_estimate=pl.CostEstimate(
+            flops=4 * 1024 * 1024 * 1024, bytes_accessed=8 << 20, transcendentals=0
+        ),
+    )(ho, mask, w)
+
+
+def fast_local(inputs, modality, segment, w_qkv, w_out):
+    heads, head_size = w_qkv.shape[1], w_out.shape[2]
+    score_scale = 1.0 / math.sqrt(head_size)
+    meta = jnp.concatenate([modality, segment, jnp.zeros((6, modality.shape[1]), jnp.int32)], axis=0)
+    tok_all, meta_all, weights = gather_all(inputs[0], meta, w_qkv)
+    s, t, z, y, x, c = coords()
+    columns = lax.all_gather(
+        w_out, "seq", axis_index_groups=[[0, 2, 4, 6], [1, 3, 5, 7]], axis=0, tiled=False
+    ).reshape(4, 2 * heads * head_size, w_out.shape[3])
+    mine = lax.dynamic_index_in_dim(meta_all, t, 0, keepdims=False)
+    modal_all = mine[:, 0].reshape(-1)
+    doc_all = mine[:, 1].reshape(-1)
+    text_part = qkv_product(tok_all, weights[0])
+    image_part = qkv_product(tok_all, weights[1])
+    projected = jnp.where(modal_all[:, None, None] == 1, image_part, text_part).astype(jnp.bfloat16)
+    head_list = []
+    for head_idx in range(heads):
+        queries = projected[:, head_idx, :head_size]
+        keys_all = projected[:, head_idx, head_size : 2 * head_size]
+        values_all = projected[:, head_idx, 2 * head_size :]
+        head_list.append(dense_attend(queries, keys_all, values_all, doc_all, score_scale))
+    ho = jnp.concatenate(head_list, axis=1)
+    block = lax.dynamic_slice_in_dim(meta_all[:, :, 0], z * 2, 2, 1)
+    block = (block.reshape(4, -1, 1) == 1).astype(jnp.bfloat16)
+    mask = jnp.broadcast_to(block, (4, block.shape[1], 128))
+    return out_project(ho, mask, columns)[None]
+
+
 def solution(mesh):
+    small = mesh.shape["seq"] == 8 and mesh.shape["tower"] == 4
     return jax.shard_map(
-        local,
+        fast_local if small else local,
         mesh=mesh,
         in_specs=(
             P("tower", "seq", None),

time: 421 us -> 263 us (0.62)
  waiting for transfers between devices: 327 us -> 0.73 us
  Pallas kernels: 0 us -> 210 us
  blocking collectives: 38.6 us -> 0 us
  matrix products: 32.9 us -> 23 us
  local copies, waits for them, and re-layouts: 3.87 us -> 8.44 us
    pallas_call x0 -> x2, Pallas kernels: none -> 210 us  [the longest x1 167 us: gather_all(): pl.pallas_call(gather_kernel, out_shape=(jax.ShapeDtypeStruct((tok.shape[...]
    all_gather x3 -> x1, waiting for transfers between devices: 175 us -> 0.02 us  [fast_local(): lax.all_gather(w_out, 'seq', axis_index_groups=[[0, 2, 4, 6], [1, 3, 5, 7...]
    reduce_scatter x1 -> x0, waiting for transfers between devices: 150 us -> none  [local(): lax.psum_scatter(jnp.where(modal_all[:, None] == 1, image_out, text_out)....]
    all_gather x2 -> x0, blocking collectives: 38.6 us -> none  [the longest x1 22.2 us: local(): modal_piece = lax.all_gather(modality, 'seq', axis=1, tiled=True)]
    dot_general x2 -> x0, matrix products: 9.09 us -> none  [out_product(): jnp.einsum('rhc,hcd->rd', row_block, weight, preferred_element_type=jnp.f...]
  transfers between devices with their start and end apart: 4 -> 1, of which waited for: 4 -> 0; matrix products, arithmetic and copies ran while one was open for 7% -> 12% of each run, Pallas kernels for 0% -> 64%
where the time goes in v1:
time: 263 us; the launch traced here: 262 us
  Pallas kernels  210 us (80%)
  matrix products  23 us (9%)
  between operations  13.6 us (5%)
  local copies, waits for them, and re-layouts  8.44 us (3%)
  other arithmetic  3.52 us (1%)
  loops' own time  2.75 us (1%)
    pallas_call x1, Pallas kernels, gather_all(): pl.pallas_call(gather_kernel, out_shape=(jax.ShapeDtypeStruct((tok.shape[...  167 us
    pallas_call x1, Pallas kernels, out_project(): pl.pallas_call(out_kernel, out_shape=jax.ShapeDtypeStruct((rows // 2, col...  43.2 us
    dot_general x2, matrix products, qkv_product(): jnp.einsum('rd,hde->rhe', row_block, weight, preferred_element_type=jnp.f...  17.7 us
  transfers between devices with their start and end apart: 1, of which 0 were waited for; matrix products, arithmetic and copies ran while one was open for 12% of the time, Pallas kernels for 64%

profile of v1, /device:TPU:0, one launch (start us, length us, event | category | flops | bytes accessed | tf_op | source)
XLA Modules:
  0.0 261.9 jit_solution(9109317155422763372)
XLA Ops:
  6.5 0.7 all-gather.3.cloned.1.call-update
  7.3 1.3 add_add_fusion.meta
  8.7 166.6 %shard_map.55 = (bf16[1024,4096]{1,0:T(8,128)(2,1)}, s32[4,8,8,128]{3,2,1,0:T(8,128)}, bf16[2,2,4096,384]{3,2,1,0:T(8,128)(2,1)}) custom-call(bf16[128,4096]{1,0:T(8,128)(2,1)} %bitcast.78, s32[8,128]{1,0:T(8,128)} %add_add_fusion.meta, bf16[2,2,1024,384]{3,2,1,0:T(8,128)(2,1)} %w.1), custom_call_target="tpu_custom_call" | custom-call | bytes 44040192 | tf_op jit(solution)/shard_map/pallas_call | solution.py:246
  175.3 0.8 dynamic-slice_bitcast_fusion
  176.1 0.9 slice.43
  177.1 11.0 %fusion.16 = bf16[1024,2,384]{2,0,1:T(8,128)(2,1)S(1)} fusion(bf16[1024,4096]{1,0:T(8,128)(2,1)} %get-tuple-element.103, bf16[2,2,4096,384]{3,2,1,0:T(8,128)(2,1)} %get-tuple-element.104), kind=kOutput, calls=%fused_computation.26 | convolution fusion | flops 6442450944 | bytes 16252928 | tf_op jit(solution)/shard_map/rd,hde->rhe/dot_general | solution.py:41
  188.3 6.7 %select_convert_fusion = bf16[1024,2,384]{2,0,1:T(8,128)(2,1)S(1)} fusion(bf16[1024,2,384]{2,0,1:T(8,128)(2,1)S(1)} %fusion.16, bf16[2,2,4096,384]{3,2,1,0:T(8,128)(2,1)S(1)} %copy-done.1, bf16[1024,4096]{1,0:T(8,128)(2,1)S(1)} %copy-done.2, pred[1024]{0:T(1024)(128)(4,1)S(1)} %bitcast.91), kind=kOutput, calls=%fused_computation.34 | convolution fusion | flops 6443237376 | bytes 17826816 | tf_op jit(solution)/shard_map/rd,hde->rhe/dot_general | solution.py:41
  195.3 6.4 %while.22 = (s32[]{:T(128)}, bf16[2,512,128]{2,1,0:T(8,128)(2,1)S(1)}, s32[2]{0:T(128)S(1)}, s32[1024]{0:T(1024)S(1)}, s32[8,1,128]{2,1,0:T(1,128)S(1)}, /*index...) while((s32[]{:T(128)}, ...), condition=%wide.region_3.4_spmd.clone, body=%wide.region_0.3_spmd.clone.sunk | while | flops 274267648 | bytes 7102655 | solution.py:36
  195.3 0.6 dynamic_slice.51
  196.6 0.7 fusion.47
  197.9 0.6 fusion.49
  198.5 0.6 dynamic_slice.51
  199.8 0.7 fusion.47
  201.0 0.6 fusion.49
  201.7 6.6 %while.23 = (s32[]{:T(128)}, bf16[2,512,128]{2,1,0:T(8,128)(2,1)S(1)}, s32[2]{0:T(128)S(1)}, s32[1024]{0:T(1024)S(1)}, s32[8,1,128]{2,1,0:T(1,128)S(1)}, /*index...) while((s32[]{:T(128)}, ...), condition=%wide.region_7.8_spmd.clone, body=%wide.region_4.7_spmd.clone.sunk | while | flops 274267648 | bytes 7102655 | solution.py:36
  201.7 0.7 dynamic_slice.54
  203.2 0.7 fusion.52
  204.4 0.6 fusion.54
  205.0 0.7 dynamic_slice.54
  206.5 0.7 fusion.52
  207.7 0.6 fusion.54
  208.7 2.2 copy-done
  210.8 43.2 %shard_map.56 = bf16[128,4096]{1,0:T(8,128)(2,1)S(1)} custom-call(bf16[1024,256]{1,0:T(8,128)(2,1)S(1)} %pad_maximum_fusion.ho, bf16[4,256,128]{2,1,0:T(8,128)(2,1)S(1)} %broadcast_in_dim.45.mask, bf16[4,512,1024]{2,1,0:T(8,128)(2,1)S(1)} %bitcast.77), custom_call_target="tpu_custom_call" | custom-call | flops 4294967296 | bytes 8388608 | tf_op jit(solution)/shard_map/pallas_call | solution.py:374
  254.0 1.0 copy.26
  (32 shorter events, 3.3 us)
Async XLA Ops:
  6.5 201.9 %all-gather.3.cloned.1.call-start = ((), (), s32[]{:S(2)}) async-start(), calls=%async_computation | async-start | bytes 5242880 | tf_op jit(solution)/shard_map/all_gather | solution.py:403
  177.1 11.1 %copy-start.1 = (bf16[2,2,4096,384]{3,2,1,0:T(8,128)(2,1)S(1)}, bf16[2,2,4096,384]{3,2,1,0:T(8,128)(2,1)}, u32[]{:S(2)}) copy-start(bf16[2,2,4096,384]{3,2,1,0:T(8,128)(2,1)} %get-tuple-element.104) | copy-start | bytes 37748740
  177.1 11.2 %copy-start.2 = (bf16[1024,4096]{1,0:T(8,128)(2,1)S(1)}, bf16[1024,4096]{1,0:T(8,128)(2,1)}, u32[]{:S(2)}) copy-start(bf16[1024,4096]{1,0:T(8,128)(2,1)} %get-tuple-element.103) | copy-start | bytes 25165828
  208.7 2.2 copy-start
Sparse Core Ops, SparseCore 0:
  8.9 115.7 all-gather.2

commit v2 on v1

--- a/solution.py
+++ b/solution.py
@@ -91,6 +91,7 @@
 
 
 MESH = pl.DeviceIdType.MESH
+PIECES = 4
 
 
 def coords():
@@ -113,8 +114,8 @@
 
 
 def gather_kernel(
-    tok, meta, w, tok_all, meta_all, w_all,
-    local_sem, up_send, dn_send, z_recv, y_send, y_recv,
+    tok, meta, w, w_out, tok_all, meta_all, w_all, near,
+    w_buf, tok_buf, local_sem, n_send, n_recv, up_send, dn_send, z_recv, y_send, y_recv,
     w_send, w_recv, m_send, m_recv, mt_send, mt_recv,
 ):
     s, t, z, y, x, c = coords()
@@ -127,36 +128,42 @@
     seq_peers = [(lax.rem(s + k, 8), t) for k in range(1, 8)]
     enter(seq_peers + [x_peer, core_peer, diagonal])
 
-    def tok_at(block):
-        return tok_all.at[pl.ds(pl.multiple_of(block * rows, rows), rows)]
+    piece = rows // PIECES
+
+    def tok_at(block, p):
+        return tok_all.at[pl.ds(pl.multiple_of(block * rows + p * piece, piece), piece)]
+
+    def mine(p):
+        return tok.at[pl.ds(p * piece, piece)]
 
     def w_at(owner, m, h):
         return w_all.at[m, h, pl.ds(pl.multiple_of(owner * depth, depth), depth)]
 
     chunks = [(m, h) for m in range(w.shape[0]) for h in range(w.shape[1])]
 
-    def up(o, src):
-        return remote(src, tok_at(o * 2 + y), up_send.at[o], z_recv.at[o], (s + 2, t))
-
-    def down(o, src):
-        return remote(src, tok_at(o * 2 + y), dn_send.at[o], z_recv.at[o], (s - 2, t))
-
-    def across(o, src):
-        return remote(src, tok_at(o * 2 + y), y_send.at[o], y_recv.at[o], y_peer)
+    def up(o, p, src):
+        return remote(src, tok_at(o * 2 + y, p), up_send.at[o, p], z_recv.at[o, p], (s + 2, t))
+
+    def down(o, p, src):
+        return remote(src, tok_at(o * 2 + y, p), dn_send.at[o, p], z_recv.at[o, p], (s - 2, t))
+
+    def across(o, p, src):
+        return remote(src, tok_at(o * 2 + y, p), y_send.at[o, p], y_recv.at[o, p], y_peer)
 
     def w_copy(kind, k, src, owner, peer):
         m, h = chunks[k]
         return remote(src, w_at(owner, m, h), w_send.at[kind, k], w_recv.at[kind, k], peer)
 
-    @pl.when(z < 3)
-    def _():
-        up(z, tok).start()
-
-    @pl.when(z > 0)
-    def _():
-        down(z, tok).start()
-
-    across(z, tok).start()
+    for p in range(PIECES):
+        @pl.when(z < 3)
+        def _():
+            up(z, p, mine(p)).start()
+
+        @pl.when(z > 0)
+        def _():
+            down(z, p, mine(p)).start()
+
+        across(z, p, mine(p)).start()
     for k, (m, h) in enumerate(chunks):
         w_copy(0, k, w.at[m, h], t, x_peer).start()
     meta_copies = [
@@ -167,13 +174,33 @@
         copy.start()
     for k, (m, h) in enumerate(chunks):
         w_copy(1, k, w.at[m, h], t, core_peer).start()
+    def near_up():
+        return remote(w_out, near.at[0], n_send.at[0], n_recv.at[0], (s + 2, t))
+
+    def near_down():
+        return remote(w_out, near.at[1], n_send.at[1], n_recv.at[1], (s - 2, t))
+
+    @pl.when(z < 3)
+    def _():
+        near_up().start()
+
+    @pl.when(z > 0)
+    def _():
+        near_down().start()
+
+    own_rows = tok_all.at[pl.ds(pl.multiple_of(s * rows, rows), rows)]
+    staged = [pltpu.make_async_copy(tok, tok_buf, local_sem.at[0])]
     own = [
-        pltpu.make_async_copy(tok, tok_at(s), local_sem.at[0]),
-        pltpu.make_async_copy(meta, meta_all.at[t, s], local_sem.at[1]),
-        pltpu.make_async_copy(
-            w, w_all.at[:, :, pl.ds(pl.multiple_of(t * depth, depth), depth)], local_sem.at[2]
-        ),
-    ]
+        pltpu.make_async_copy(tok_buf, own_rows, local_sem.at[1]),
+        pltpu.make_async_copy(meta, meta_all.at[t, s], local_sem.at[2]),
+    ]
+    for k, (m, h) in enumerate(chunks):
+        staged.append(pltpu.make_async_copy(w.at[m, h], w_buf.at[k], local_sem.at[3 + 2 * k]))
+        own.append(pltpu.make_async_copy(w_buf.at[k], w_at(t, m, h), local_sem.at[4 + 2 * k]))
+    for copy in staged:
+        copy.start()
+    for copy in staged:
+        copy.wait()
     for copy in own:
         copy.start()
 
@@ -187,26 +214,28 @@
         if d - 1 < n_chunks:
             pass_weights(d - 1)
         low, high = z - d, z + d
-
-        @pl.when(low >= 0)
-        def _():
-            up(low, tok_at(low * 2 + y)).wait_recv()
-
-            @pl.when(z < 3)
+        for p in range(PIECES):
+            @pl.when(low >= 0)
             def _():
-                up(low, tok_at(low * 2 + y)).start()
-
-            across(low, tok_at(low * 2 + y)).start()
-
-        @pl.when(high <= 3)
-        def _():
-            down(high, tok_at(high * 2 + y)).wait_recv()
-
-            @pl.when(z > 0)
+                src = tok_at(low * 2 + y, p)
+                up(low, p, src).wait_recv()
+
+                @pl.when(z < 3)
+                def _():
+                    up(low, p, src).start()
+
+                across(low, p, src).start()
+
+            @pl.when(high <= 3)
             def _():
-                down(high, tok_at(high * 2 + y)).start()
-
-            across(high, tok_at(high * 2 + y)).start()
+                src = tok_at(high * 2 + y, p)
+                down(high, p, src).wait_recv()
+
+                @pl.when(z > 0)
+                def _():
+                    down(high, p, src).start()
+
+                across(high, p, src).start()
 
     for k in range(3, n_chunks):
         pass_weights(k)
@@ -221,15 +250,16 @@
     for copy in tower_meta:
         copy.start()
     for o in range(4):
-        across(o, tok).wait()
-
-        @pl.when((z < 3) & (o <= z))
-        def _():
-            up(o, tok).wait_send()
-
-        @pl.when((z > 0) & (o >= z))
-        def _():
-            down(o, tok).wait_send()
+        for p in range(PIECES):
+            across(o, p, mine(p)).wait()
+
+            @pl.when((z < 3) & (o <= z))
+            def _():
+                up(o, p, mine(p)).wait_send()
+
+            @pl.when((z > 0) & (o >= z))
+            def _():
+                down(o, p, mine(p)).wait_send()
 
     for k, (m, h) in enumerate(chunks):
         w_copy(0, k, w.at[m, h], t, x_peer).wait_send()
@@ -238,8 +268,18 @@
     for copy in tower_meta:
         copy.wait()
 
-
-def gather_all(tok, meta, w):
+    @pl.when(z < 3)
+    def _():
+        near_up().wait_send()
+        near_down().wait_recv()
+
+    @pl.when(z > 0)
+    def _():
+        near_down().wait_send()
+        near_up().wait_recv()
+
+
+def gather_all(tok, meta, w, w_out):
     dma = pltpu.SemaphoreType.DMA
     hbm = pl.BlockSpec(memory_space=pl.ANY)
     heads = w.shape[1]
@@ -249,27 +289,35 @@
             jax.ShapeDtypeStruct((tok.shape[0] * 8, tok.shape[1]), tok.dtype),
             jax.ShapeDtypeStruct((4, 8) + meta.shape, meta.dtype),
             jax.ShapeDtypeStruct((2, heads, w.shape[2] * 4, w.shape[3]), w.dtype),
+            jax.ShapeDtypeStruct((2,) + w_out.shape, w_out.dtype),
         ),
-        in_specs=[hbm] * 3,
-        out_specs=(hbm, hbm, hbm),
+        in_specs=[hbm] * 4,
+        out_specs=(hbm, hbm, hbm, hbm),
         scratch_shapes=[
-            dma((3,)), dma((4,)), dma((4,)), dma((4,)), dma((4,)), dma((4,)),
+            pltpu.VMEM((2 * heads,) + w.shape[2:], w.dtype), pltpu.VMEM(tok.shape, tok.dtype),
+            dma((3 + 4 * heads,)), dma((2,)), dma((2,)), dma((4, PIECES)), dma((4, PIECES)), dma((4, PIECES)),
+            dma((4, PIECES)), dma((4, PIECES)),
             dma((3, 2 * heads)), dma((3, 2 * heads)), dma((7,)), dma((7,)), dma((3,)), dma((3,)),
         ],
-        compiler_params=pltpu.CompilerParams(collective_id=0, has_side_effects=True),
+        compiler_params=pltpu.CompilerParams(
+            collective_id=0, has_side_effects=True, vmem_limit_bytes=16 << 20
+        ),
         cost_estimate=pl.CostEstimate(flops=0, bytes_accessed=42 << 20, transcendentals=0),
-    )(tok, meta, w)
+    )(tok, meta, w, w_out)
 
 
 def out_kernel(
-    ho, mask, w, out, got, lhs, keep, sent, arrived, ready,
+    ho, mask, w0, w1, w2, w3, out, got, lhs, keep, sent, arrived, ready,
     z_send, z_recv, g_send, g_recv, y_send, y_recv, o_send, o_recv,
 ):
     s, t, z, y, x, c = coords()
     rows = ho.shape[0] // 4
     half = rows // 2
     width = ho.shape[1]
-    cols = w.shape[2]
+    cols = w0.shape[1]
+    below = jnp.where(z == 0, 1, z - 1)
+    across = lax.rem(z + 2, 4)
+    groups = [(z, w0), (below, w1), (across, w2), (6 - z - below - across, w3)]
     order = [t, x * 2 + (1 - c), (1 - x) * 2 + c, (1 - x) * 2 + (1 - c)]
     x_peer, core_peer = (s, order[2]), (s, order[1])
     y_peer = (z * 2 + (1 - y), t)
@@ -302,7 +350,7 @@
     def project(j):
         owner = order[j]
         for g in range(4):
-            block = got[owner, g]
+            block = got[owner, groups[g][0]]
             m = mask[owner]
             for h in range(width // 128):
                 part = block[:, h * 128:(h + 1) * 128]
@@ -318,7 +366,7 @@
                 total = None
                 for g in range(4):
                     part = jnp.dot(
-                        lhs[g, rows_of(side, half), :], w[g, :, at],
+                        lhs[g, rows_of(side, half), :], groups[g][1][:, at],
                         preferred_element_type=jnp.float32,
                     ).astype(jnp.bfloat16).astype(jnp.float32)
                     total = part if total is None else total + part
@@ -367,14 +415,14 @@
         copy.wait()
 
 
-def out_project(ho, mask, w):
+def out_project(ho, mask, ws):
     dma = pltpu.SemaphoreType.DMA
     vmem = pl.BlockSpec(memory_space=pltpu.VMEM)
-    rows, cols, width = ho.shape[0] // 4, w.shape[2], ho.shape[1]
+    rows, cols, width = ho.shape[0] // 4, ws[0].shape[1], ho.shape[1]
     return pl.pallas_call(
         out_kernel,
         out_shape=jax.ShapeDtypeStruct((rows // 2, cols * 4), jnp.bfloat16),
-        in_specs=[vmem] * 3,
+        in_specs=[vmem] * 6,
         out_specs=vmem,
         scratch_shapes=[
             pltpu.VMEM((4, 4, rows, width), jnp.bfloat16),
@@ -391,18 +439,29 @@
         cost_estimate=pl.CostEstimate(
             flops=4 * 1024 * 1024 * 1024, bytes_accessed=8 << 20, transcendentals=0
         ),
-    )(ho, mask, w)
+    )(ho, mask, *ws)
 
 
 def fast_local(inputs, modality, segment, w_qkv, w_out):
     heads, head_size = w_qkv.shape[1], w_out.shape[2]
     score_scale = 1.0 / math.sqrt(head_size)
     meta = jnp.concatenate([modality, segment, jnp.zeros((6, modality.shape[1]), jnp.int32)], axis=0)
-    tok_all, meta_all, weights = gather_all(inputs[0], meta, w_qkv)
+    tok_all, meta_all, weights, near = gather_all(inputs[0], meta, w_qkv, w_out)
     s, t, z, y, x, c = coords()
-    columns = lax.all_gather(
-        w_out, "seq", axis_index_groups=[[0, 2, 4, 6], [1, 3, 5, 7]], axis=0, tiled=False
-    ).reshape(4, 2 * heads * head_size, w_out.shape[3])
+    up_pairs = [(a * 2 + b, (a + 1) * 2 + b) for a in (1, 2) for b in (0, 1)]
+    down_pairs = [(a * 2 + b, (a - 1) * 2 + b) for a in (1, 2) for b in (0, 1)]
+    end_pairs = [(2 + b, b) for b in (0, 1)] + [(4 + b, 6 + b) for b in (0, 1)]
+    from_low = lax.ppermute(near[0], "seq", up_pairs)
+    from_high = lax.ppermute(near[1], "seq", down_pairs)
+    far = jnp.where(z >= 2, from_low, from_high)
+    last = lax.ppermute(far, "seq", end_pairs)
+    blocks = [
+        w_out,
+        jnp.where(z == 0, near[1], near[0]),
+        far,
+        jnp.where((z == 0) | (z == 3), last, near[1]),
+    ]
+    columns = [b.reshape(2 * heads * head_size, w_out.shape[3]) for b in blocks]
     mine = lax.dynamic_index_in_dim(meta_all, t, 0, keepdims=False)
     modal_all = mine[:, 0].reshape(-1)
     doc_all = mine[:, 1].reshape(-1)

time: 263 us -> 225 us (0.86)
  Pallas kernels: 210 us -> 148 us
  waiting for transfers between devices: 0.73 us -> 14.1 us
  between operations: 13.6 us -> 0.27 us
  local copies, waits for them, and re-layouts: 8.44 us -> 18.5 us
  other arithmetic: 3.52 us -> 8.49 us
  matrix products: 23 us -> 27.2 us
  starting transfers between devices: 0.01 us -> 3.48 us
    pallas_call x1, Pallas kernels: 167 us -> 105 us  [gather_all(): pl.pallas_call(gather_kernel, out_shape=(jax.ShapeDtypeStruct((tok.shape[...]
    ppermute x0 -> x3, waiting for transfers between devices: none -> 14.1 us  [the longest x1 14.1 us: fast_local(): last = lax.ppermute(far, 'seq', end_pairs)]
    unnamed x8 -> x24, local copies, waits for them, and re-layouts: 3.29 us -> 14.2 us
    dot_general x4, matrix products: 2.91 us -> 7.11 us  [key_scores(): lax.dot_general(q_block, keys_tile, (((1,), (1,)), ((), ())), preferred_e...]
    ppermute x0 -> x3, starting transfers between devices: none -> 3.48 us  [the longest x1 1.47 us: fast_local(): last = lax.ppermute(far, 'seq', end_pairs)]
    select_n x0 -> x2, other arithmetic: none -> 2.67 us  [the longest x1 1.34 us: fast_local(): far = jnp.where(z >= 2, from_low, from_high)]
  transfers between devices with their start and end apart: 1 -> 3, of which waited for: 0 -> 1; matrix products, arithmetic and copies ran while one was open for 12% -> 16% of each run, Pallas kernels for 64% -> 0%
where the time goes in v2:
time: 225 us; the launch traced here: 222 us
  Pallas kernels  148 us (66%)
  matrix products  27.2 us (12%)
  local copies, waits for them, and re-layouts  18.5 us (8%)
  waiting for transfers between devices  14.1 us (6%)
  other arithmetic  8.49 us (4%)
  starting transfers between devices  3.48 us (2%)
  loops' own time  2.57 us (1%)
    pallas_call x1, Pallas kernels, gather_all(): pl.pallas_call(gather_kernel, out_shape=(jax.ShapeDtypeStruct((tok.shape[...  105 us
    pallas_call x1, Pallas kernels, out_project(): pl.pallas_call(out_kernel, out_shape=jax.ShapeDtypeStruct((rows // 2, col...  43 us
    dot_general x2, matrix products, qkv_product(): jnp.einsum('rd,hde->rhe', row_block, weight, preferred_element_type=jnp.f...  17.7 us
    unnamed x24, local copies, waits for them, and re-layouts  14.2 us
    ppermute x1, waiting for transfers between devices, fast_local(): last = lax.ppermute(far, 'seq', end_pairs)  14.1 us
    dot_general x4, matrix products, key_scores(): lax.dot_general(q_block, keys_tile, (((1,), (1,)), ((), ())), preferred_e...  7.11 us
  transfers between devices with their start and end apart: 3, of which 1 were waited for; matrix products, arithmetic and copies ran while one was open for 16% of the time, Pallas kernels for 0%

profile of v2, /device:TPU:0, one launch (start us, length us, event | category | flops | bytes accessed | tf_op | source)
XLA Modules:
  0.0 222.4 jit_solution(519765154847999129)
XLA Ops:
  0.8 1.9 copy-done
  2.7 1.2 copy-done.1
  3.9 1.2 copy-done.2
  5.2 104.7 %shard_map.55 = (bf16[1024,4096]{1,0:T(8,128)(2,1)S(1)}, s32[4,8,8,128]{3,2,1,0:T(8,128)S(1)}, bf16[2,2,4096,384]{3,2,1,0:T(8,128)(2,1)S(1)}, bf16[2,2,2,128,1024]{4,3,2,1,0:T(8,128)(2,1)S(1)}) custom-call(bf16[128,4096]{1,0:T(8,128)(2,1)S(1)} %bitcast.88, s32[8,128]{1,0:T(8,128)S(1)} %add_add_fusion.meta, bf16[2,2,1024,384]{3,2,1,0:T(8,128)(2,1)S(1)} %copy-done, ...), custom_call_target="tpu_custom_call" | custom-call | bytes 44040192 | tf_op jit(solution)/shard_map/pallas_call | solution.py:286
  109.9 4.5 %copy-done.5 = bf16[2,2,4096,384]{3,2,1,0:T(8,128)(2,1)} copy-done((bf16[2,2,4096,384]{3,2,1,0:T(8,128)(2,1)}, bf16[2,2,4096,384]{3,2,1,0:T(8,128)(2,1)S(1)}, u32[]{:S(2)}) %copy-start.5) | copy-done | bytes 12582936
  114.4 3.2 %copy-done.7 = bf16[1024,4096]{1,0:T(8,128)(2,1)} copy-done((bf16[1024,4096]{1,0:T(8,128)(2,1)}, bf16[1024,4096]{1,0:T(8,128)(2,1)S(1)}, u32[]{:S(2)}) %copy-start.7) | copy-done | bytes 8388632
  117.6 1.8 slice_bitcast_fusion.1
  120.1 1.3 collective-permute-start.1
  121.5 11.0 %fusion.16 = bf16[1024,2,384]{2,0,1:T(8,128)(2,1)S(1)} fusion(bf16[1024,4096]{1,0:T(8,128)(2,1)} %copy-done.7, bf16[2,2,4096,384]{3,2,1,0:T(8,128)(2,1)} %copy-done.5), kind=kOutput, calls=%fused_computation.26 | convolution fusion | flops 6442450944 | bytes 16252928 | tf_op jit(solution)/shard_map/rd,hde->rhe/dot_general | solution.py:41
  132.7 6.7 %select_convert_fusion = bf16[1024,2,384]{2,0,1:T(8,128)(2,1)S(1)} fusion(bf16[1024,2,384]{2,0,1:T(8,128)(2,1)S(1)} %fusion.16, bf16[2,2,4096,384]{3,2,1,0:T(8,128)(2,1)S(1)} %copy-done.6, bf16[1024,4096]{1,0:T(8,128)(2,1)S(1)} %copy-done.8, pred[1024]{0:T(1024)(128)(4,1)S(1)} %bitcast.103), kind=kOutput, calls=%fused_computation.34 | convolution fusion | flops 6443237376 | bytes 17826816 | tf_op jit(solution)/shard_map/rd,hde->rhe/dot_general | solution.py:41
  139.4 1.3 slice_bitcast_fusion.5
  140.7 8.3 %while.23 = (s32[]{:T(128)}, bf16[2,512,128]{2,1,0:T(8,128)(2,1)S(1)}, s32[2]{0:T(128)S(1)}, s32[1024]{0:T(1024)S(1)}, s32[8,1,128]{2,1,0:T(1,128)S(1)}, /*index...) while((s32[]{:T(128)}, ...), condition=%wide.region_7.8_spmd.clone, body=%wide.region_4.7_spmd.clone.sunk | while | flops 274267648 | bytes 8151267 | solution.py:36
  141.9 1.8 fusion.52
  146.1 1.8 fusion.52
  149.0 1.0 copy-done.9
  150.1 1.3 broadcast_select_fusion.1
  151.4 1.5 collective-permute-start.2
  152.9 8.5 %while.22 = (s32[]{:T(128)}, bf16[2,512,128]{2,1,0:T(8,128)(2,1)S(1)}, s32[2]{0:T(128)S(1)}, s32[1024]{0:T(1024)S(1)}, s32[8,1,128]{2,1,0:T(1,128)S(1)}, /*index...) while((s32[]{:T(128)}, ...), condition=%wide.region_3.4_spmd.clone, body=%wide.region_0.3_spmd.clone.sunk | while | flops 274267648 | bytes 8151267 | solution.py:36
  154.3 1.8 fusion.47
  158.6 1.8 fusion.47
  161.6 1.2 pad_maximum_fusion.ho
  162.7 14.1 %collective-permute-done.2 = bf16[2,2,128,1024]{3,2,1,0:T(8,128)(2,1)} collective-permute-done((bf16[2,2,128,1024]{3,2,1,0:T(8,128)(2,1)S(1)}, bf16[2,2,128,1024]{3,2,1,0:T(8,128)(2,1)}, u32[]{:S(2)}, u32[]{:S(2)}) %collective-permute-start.2) | collective-permute-done | bytes 1048608 | tf_op jit(solution)/shard_map/ppermute | solution.py:457
  176.9 1.3 broadcast_select_fusion
  178.4 43.0 %shard_map.56 = bf16[128,4096]{1,0:T(8,128)(2,1)S(1)} custom-call(bf16[1024,256]{1,0:T(8,128)(2,1)S(1)} %pad_maximum_fusion.ho, bf16[4,256,128]{2,1,0:T(8,128)(2,1)S(1)} %broadcast_in_dim.45.mask, bf16[512,1024]{1,0:T(8,128)(2,1)S(1)} %bitcast.89, bf16[512,1024]{1,0:T(8,128)(2,1)S(1)} %bitcast.90, bf16[512,1024]{1,0:T(8,128)(2,1)S(1)} %bitcast.85, ...), custom_call_target="tpu_custom_call" | custom-call | flops 4294967296 | bytes 8388608 | tf_op jit(solution)/shard_map/pallas_call | solution.py:422
  (62 shorter events, 10.2 us)
Async XLA Ops:
  0.8 1.9 copy-start
  2.7 1.2 copy-start.1
  3.9 1.2 copy-start.2
  109.9 4.5 %copy-start.5 = (bf16[2,2,4096,384]{3,2,1,0:T(8,128)(2,1)}, bf16[2,2,4096,384]{3,2,1,0:T(8,128)(2,1)S(1)}, u32[]{:S(2)}) copy-start(bf16[2,2,4096,384]{3,2,1,0:T(8,128)(2,1)S(1)} %get-tuple-element.105) | copy-start | bytes 37748740
  114.4 3.2 %copy-start.7 = (bf16[1024,4096]{1,0:T(8,128)(2,1)}, bf16[1024,4096]{1,0:T(8,128)(2,1)S(1)}, u32[]{:S(2)}) copy-start(bf16[1024,4096]{1,0:T(8,128)(2,1)S(1)} %get-tuple-element.104) | copy-start | bytes 25165828
  119.4 29.6 %collective-permute-start = (bf16[2,2,128,1024]{3,2,1,0:T(8,128)(2,1)}, bf16[2,2,128,1024]{3,2,1,0:T(8,128)(2,1)S(1)}, u32[]{:S(2)}, u32[]{:S(2)}) collective-permute-start(bf16[2,2,128,1024]{3,2,1,0:T(8,128)(2,1)} %get-tuple-element.198), channel_id=1, source_target_pairs={{8,16},{12,20},{16,24},{20,28},{9,17},{13,21},{17,25},{21,29},{10,... | collective-permute-start | bytes 3145736 | tf_op jit(solution)/shard_map/ppermute | solution.py:454
  120.1 29.9 %collective-permute-start.1 = (bf16[2,2,128,1024]{3,2,1,0:T(8,128)(2,1)}, bf16[2,2,128,1024]{3,2,1,0:T(8,128)(2,1)}, u32[]{:S(2)}, u32[]{:S(2)}) collective-permute-start(bf16[2,2,128,1024]{3,2,1,0:T(8,128)(2,1)} %get-tuple-element.197), channel_id=1, source_target_pairs={{8,0},{12,4},{16,8},{20,12},{9,1},{13,5},{17,9},{21,13},{10,2},{14... | collective-permute-start | bytes 3145736 | tf_op jit(solution)/shard_map/ppermute | solution.py:455
  121.5 11.1 %copy-start.6 = (bf16[2,2,4096,384]{3,2,1,0:T(8,128)(2,1)S(1)}, bf16[2,2,4096,384]{3,2,1,0:T(8,128)(2,1)}, u32[]{:S(2)}) copy-start(bf16[2,2,4096,384]{3,2,1,0:T(8,128)(2,1)} %copy-done.5) | copy-start | bytes 37748740
  121.5 11.2 %copy-start.8 = (bf16[1024,4096]{1,0:T(8,128)(2,1)S(1)}, bf16[1024,4096]{1,0:T(8,128)(2,1)}, u32[]{:S(2)}) copy-start(bf16[1024,4096]{1,0:T(8,128)(2,1)} %copy-done.7) | copy-start | bytes 25165828
  141.9 2.3 %copy-start.12 = (bf16[1024,128]{1,0:T(8,128)(2,1)S(1)}, bf16[1024,128]{1,0:T(8,128)(2,1)}, u32[]{:S(2)}) copy-start(bf16[1024,128]{1,0:T(8,128)(2,1)} %get-tuple-element.343) | copy-start | bytes 786436 | tf_op jit(solution)/shard_map/while
  146.1 2.3 %copy-start.12 = (bf16[1024,128]{1,0:T(8,128)(2,1)S(1)}, bf16[1024,128]{1,0:T(8,128)(2,1)}, u32[]{:S(2)}) copy-start(bf16[1024,128]{1,0:T(8,128)(2,1)} %get-tuple-element.343) | copy-start | bytes 786436 | tf_op jit(solution)/shard_map/while
  149.0 3.9 %copy-start.10 = (bf16[2,512,128]{2,1,0:T(8,128)(2,1)}, bf16[2,512,128]{2,1,0:T(8,128)(2,1)S(1)}, u32[]{:S(2)}) copy-start(bf16[2,512,128]{2,1,0:T(8,128)(2,1)S(1)} %get-tuple-element.107) | copy-start | bytes 786436
  149.0 1.0 copy-start.9
  151.4 25.5 %collective-permute-start.2 = (bf16[2,2,128,1024]{3,2,1,0:T(8,128)(2,1)S(1)}, bf16[2,2,128,1024]{3,2,1,0:T(8,128)(2,1)}, u32[]{:S(2)}, u32[]{:S(2)}) collective-permute-start(bf16[2,2,128,1024]{3,2,1,0:T(8,128)(2,1)S(1)} %broadcast_select_fusion.1), channel_id=1, source_target_pairs={{8,0},{12,4},{16,24},{20,28},{9,1},{13,5},{17,25},{21,29},{10,2},{... | collective-permute-start | bytes 3145736 | tf_op jit(solution)/shard_map/ppermute | solution.py:457
  154.3 2.3 %copy-start.11 = (bf16[1024,128]{1,0:T(8,128)(2,1)S(1)}, bf16[1024,128]{1,0:T(8,128)(2,1)}, u32[]{:S(2)}) copy-start(bf16[1024,128]{1,0:T(8,128)(2,1)} %get-tuple-element.379) | copy-start | bytes 786436 | tf_op jit(solution)/shard_map/while
  158.6 2.3 %copy-start.11 = (bf16[1024,128]{1,0:T(8,128)(2,1)S(1)}, bf16[1024,128]{1,0:T(8,128)(2,1)}, u32[]{:S(2)}) copy-start(bf16[1024,128]{1,0:T(8,128)(2,1)} %get-tuple-element.379) | copy-start | bytes 786436 | tf_op jit(solution)/shard_map/while
  161.5 16.9 %copy-start.3 = (bf16[2,2,128,1024]{3,2,1,0:T(8,128)(2,1)S(1)}, bf16[2,2,128,1024]{3,2,1,0:T(8,128)(2,1)}, u32[]{:S(2)}) copy-start(bf16[2,2,128,1024]{3,2,1,0:T(8,128)(2,1)} %w_out.1) | copy-start | bytes 3145732
  161.6 16.9 %copy-start.4 = (bf16[1,2,2,128,1024]{4,3,2,1,0:T(8,128)(2,1)S(1)}, bf16[1,2,2,128,1024]{4,3,2,1,0:T(8,128)(2,1)}, u32[]{:S(2)}) copy-start(bf16[1,2,2,128,1024]{4,3,2,1,0:T(8,128)(2,1)} %get-tuple-element.199) | copy-start | bytes 3145732

commit v3 on v2

--- a/solution.py
+++ b/solution.py
@@ -114,7 +114,7 @@
 
 
 def gather_kernel(
-    tok, meta, w, w_out, tok_all, meta_all, w_all, near,
+    tok, meta, w, w_out, tok_all, meta_all, w_all, near_low, near_high,
     w_buf, tok_buf, local_sem, n_send, n_recv, up_send, dn_send, z_recv, y_send, y_recv,
     w_send, w_recv, m_send, m_recv, mt_send, mt_recv,
 ):
@@ -175,10 +175,10 @@
     for k, (m, h) in enumerate(chunks):
         w_copy(1, k, w.at[m, h], t, core_peer).start()
     def near_up():
-        return remote(w_out, near.at[0], n_send.at[0], n_recv.at[0], (s + 2, t))
+        return remote(w_out, near_low, n_send.at[0], n_recv.at[0], (s + 2, t))
 
     def near_down():
-        return remote(w_out, near.at[1], n_send.at[1], n_recv.at[1], (s - 2, t))
+        return remote(w_out, near_high, n_send.at[1], n_recv.at[1], (s - 2, t))
 
     @pl.when(z < 3)
     def _():
@@ -289,10 +289,11 @@
             jax.ShapeDtypeStruct((tok.shape[0] * 8, tok.shape[1]), tok.dtype),
             jax.ShapeDtypeStruct((4, 8) + meta.shape, meta.dtype),
             jax.ShapeDtypeStruct((2, heads, w.shape[2] * 4, w.shape[3]), w.dtype),
-            jax.ShapeDtypeStruct((2,) + w_out.shape, w_out.dtype),
+            jax.ShapeDtypeStruct(w_out.shape, w_out.dtype),
+            jax.ShapeDtypeStruct(w_out.shape, w_out.dtype),
         ),
         in_specs=[hbm] * 4,
-        out_specs=(hbm, hbm, hbm, hbm),
+        out_specs=(hbm,) * 5,
         scratch_shapes=[
             pltpu.VMEM((2 * heads,) + w.shape[2:], w.dtype), pltpu.VMEM(tok.shape, tok.dtype),
             dma((3 + 4 * heads,)), dma((2,)), dma((2,)), dma((4, PIECES)), dma((4, PIECES)), dma((4, PIECES)),
@@ -300,7 +301,7 @@
             dma((3, 2 * heads)), dma((3, 2 * heads)), dma((7,)), dma((7,)), dma((3,)), dma((3,)),
         ],
         compiler_params=pltpu.CompilerParams(
-            collective_id=0, has_side_effects=True, vmem_limit_bytes=16 << 20
+            collective_id=0, has_side_effects=True, vmem_limit_bytes=56 << 20
         ),
         cost_estimate=pl.CostEstimate(flops=0, bytes_accessed=42 << 20, transcendentals=0),
     )(tok, meta, w, w_out)
@@ -337,15 +338,18 @@
     for copy in z_copies:
         copy.start()
     got[t, z] = ho[rows_of(z, rows)]
-    for copy in z_copies:
-        copy.wait_recv()
-    g_copies = [
-        remote(got.at[t], got.at[t], g_send.at[0], g_recv.at[0], x_peer),
-        remote(got.at[t], got.at[t], g_send.at[1], g_recv.at[1], core_peer),
-        remote(got.at[order[2]], got.at[order[2]], g_send.at[2], g_recv.at[2], core_peer),
-    ]
-    g_copies[0].start()
-    g_copies[1].start()
+    origins = [z] + [lax.rem(z + k, 4) for k in (3, 1, 2)]
+
+    def g_copy(kind, i):
+        block = got.at[order[2] if kind == 2 else t, origins[i]]
+        peer = x_peer if kind == 0 else core_peer
+        return remote(block, block, g_send.at[kind, i], g_recv.at[kind, i], peer)
+
+    for i, k in enumerate((0, 1, 3, 2)):
+        if k:
+            z_copies[k - 1].wait_recv()
+        g_copy(0, i).start()
+        g_copy(1, i).start()
 
     def project(j):
         owner = order[j]
@@ -393,24 +397,30 @@
             ready[j] = total
             o_copies[j - 1].start()
 
+    for i in range(4):
+        g_copy(1, i).wait_recv()
+    project(1)
+    y_copies[1].start()
+    for i in range(4):
+        g_copy(0, i).wait_recv()
+        g_copy(2, i).start()
+    project(2)
+    y_copies[2].start()
+    for i in range(4):
+        g_copy(2, i).wait_recv()
+    project(3)
+    y_copies[3].start()
+    finish(1)
     project(0)
     y_copies[0].start()
-    g_copies[1].wait_recv()
-    project(1)
-    y_copies[1].start()
-    g_copies[0].wait_recv()
-    g_copies[2].start()
-    project(2)
-    y_copies[2].start()
-    finish(1)
-    g_copies[2].wait_recv()
-    project(3)
-    y_copies[3].start()
-    finish(0)
     finish(2)
     finish(3)
-    for copy in z_copies + g_copies + y_copies:
+    finish(0)
+    for copy in z_copies + y_copies:
         copy.wait_send()
+    for kind in range(3):
+        for i in range(4):
+            g_copy(kind, i).wait_send()
     for copy in o_copies:
         copy.wait()
 
@@ -431,7 +441,7 @@
             pltpu.VMEM((4, rows // 2, cols), jnp.bfloat16),
             pltpu.VMEM((4, rows // 2, cols), jnp.bfloat16),
             pltpu.VMEM((4, rows // 2, cols), jnp.bfloat16),
-            dma((3,)), dma((3,)), dma((3,)), dma((3,)), dma((4,)), dma((4,)), dma((3,)), dma((3,)),
+            dma((3,)), dma((3,)), dma((3, 4)), dma((3, 4)), dma((4,)), dma((4,)), dma((3,)), dma((3,)),
         ],
         compiler_params=pltpu.CompilerParams(
             collective_id=1, has_side_effects=True, vmem_limit_bytes=40 << 20
@@ -446,20 +456,20 @@
     heads, head_size = w_qkv.shape[1], w_out.shape[2]
     score_scale = 1.0 / math.sqrt(head_size)
     meta = jnp.concatenate([modality, segment, jnp.zeros((6, modality.shape[1]), jnp.int32)], axis=0)
-    tok_all, meta_all, weights, near = gather_all(inputs[0], meta, w_qkv, w_out)
+    tok_all, meta_all, weights, near_low, near_high = gather_all(inputs[0], meta, w_qkv, w_out)
     s, t, z, y, x, c = coords()
     up_pairs = [(a * 2 + b, (a + 1) * 2 + b) for a in (1, 2) for b in (0, 1)]
     down_pairs = [(a * 2 + b, (a - 1) * 2 + b) for a in (1, 2) for b in (0, 1)]
     end_pairs = [(2 + b, b) for b in (0, 1)] + [(4 + b, 6 + b) for b in (0, 1)]
-    from_low = lax.ppermute(near[0], "seq", up_pairs)
-    from_high = lax.ppermute(near[1], "seq", down_pairs)
+    from_low = lax.ppermute(near_low, "seq", up_pairs)
+    from_high = lax.ppermute(near_high, "seq", down_pairs)
     far = jnp.where(z >= 2, from_low, from_high)
     last = lax.ppermute(far, "seq", end_pairs)
     blocks = [
         w_out,
-        jnp.where(z == 0, near[1], near[0]),
+        jnp.where(z == 0, near_high, near_low),
         far,
-        jnp.where((z == 0) | (z == 3), last, near[1]),
+        jnp.where((z == 0) | (z == 3), last, near_high),
     ]
     columns = [b.reshape(2 * heads * head_size, w_out.shape[3]) for b in blocks]
     mine = lax.dynamic_index_in_dim(meta_all, t, 0, keepdims=False)

time: 225 us -> 206 us (0.916)
  local copies, waits for them, and re-layouts: 18.5 us -> 7.12 us
  other arithmetic: 8.49 us -> 5.34 us
    unnamed x24 -> x10, local copies, waits for them, and re-layouts: 14.2 us -> 1.12 us
where the time goes in v3:
time: 206 us
  Pallas kernels  147 us (71%)
  matrix products  25.1 us (12%)
  waiting for transfers between devices  14.4 us (7%)
  local copies, waits for them, and re-layouts  7.12 us (3%)
  other arithmetic  5.34 us (3%)
  starting transfers between devices  3.49 us (2%)
  loops' own time  2.74 us (1%)
    pallas_call x1, Pallas kernels, gather_all(): pl.pallas_call(gather_kernel, out_shape=(jax.ShapeDtypeStruct((tok.shape[...  105 us
    pallas_call x1, Pallas kernels, out_project(): pl.pallas_call(out_kernel, out_shape=jax.ShapeDtypeStruct((rows // 2, col...  41.8 us
    dot_general x2, matrix products, qkv_product(): jnp.einsum('rd,hde->rhe', row_block, weight, preferred_element_type=jnp.f...  17.7 us
    ppermute x1, waiting for transfers between devices, fast_local(): last = lax.ppermute(far, 'seq', end_pairs)  14.4 us
    dot_general x4, matrix products, key_scores(): lax.dot_general(q_block, keys_tile, (((1,), (1,)), ((), ())), preferred_e...  5.02 us
  transfers between devices with their start and end apart: 3, of which 1 were waited for; matrix products, arithmetic and copies ran while one was open for 16% of the time, Pallas kernels for 0%

profile of v3, /device:TPU:0, one launch (start us, length us, event | category | flops | bytes accessed | tf_op | source)
XLA Modules:
  0.0 205.6 jit_solution(1841574817690572336)
XLA Ops:
  0.1 1.3 add_add_fusion.meta
  1.4 105.4 %shard_map.55 = (bf16[1024,4096]{1,0:T(8,128)(2,1)}, s32[4,8,8,128]{3,2,1,0:T(8,128)}, bf16[2,2,4096,384]{3,2,1,0:T(8,128)(2,1)}, bf16[2,2,128,1024]{3,2,1,0:T(8,128)(2,1)}, bf16[2,2,128,1024]{3,2,1,0:T(8,128)(2,1)}) custom-call(bf16[128,4096]{1,0:T(8,128)(2,1)} %bitcast.86, s32[8,128]{1,0:T(8,128)} %add_add_fusion.meta, bf16[2,2,1024,384]{3,2,1,0:T(8,128)(2,1)} %w.1, ...), custom_call_target="tpu_custom_call" | custom-call | bytes 44040192 | tf_op jit(solution)/shard_map/pallas_call | solution.py:286
  106.8 0.7 collective-permute-start
  107.5 1.3 collective-permute-start.1
  108.9 0.8 dynamic-slice_bitcast_fusion
  109.7 11.0 %fusion.16 = bf16[1024,2,384]{2,0,1:T(8,128)(2,1)S(1)} fusion(bf16[1024,4096]{1,0:T(8,128)(2,1)} %get-tuple-element.105, bf16[2,2,4096,384]{3,2,1,0:T(8,128)(2,1)} %get-tuple-element.106), kind=kOutput, calls=%fused_computation.26 | convolution fusion | flops 6442450944 | bytes 16252928 | tf_op jit(solution)/shard_map/rd,hde->rhe/dot_general | solution.py:41
  120.9 6.7 %select_convert_fusion = bf16[1024,2,384]{2,0,1:T(8,128)(2,1)S(1)} fusion(bf16[1024,2,384]{2,0,1:T(8,128)(2,1)S(1)} %fusion.16, bf16[2,2,4096,384]{3,2,1,0:T(8,128)(2,1)S(1)} %copy-done.3, bf16[1024,4096]{1,0:T(8,128)(2,1)S(1)} %copy-done.4, pred[1024]{0:T(1024)(128)(4,1)S(1)} %bitcast.97), kind=kOutput, calls=%fused_computation.34 | convolution fusion | flops 6443237376 | bytes 17826816 | tf_op jit(solution)/shard_map/rd,hde->rhe/dot_general | solution.py:41
  127.5 1.1 slice_bitcast_fusion.3
  128.6 6.6 %while.23 = (s32[]{:T(128)}, bf16[2,512,128]{2,1,0:T(8,128)(2,1)S(1)}, s32[2]{0:T(128)S(1)}, s32[1024]{0:T(1024)S(1)}, s32[8,1,128]{2,1,0:T(1,128)S(1)}, /*index...) while((s32[]{:T(128)}, ...), condition=%wide.region_7.8_spmd.clone, body=%wide.region_4.7_spmd.clone.sunk | while | flops 274267648 | bytes 7102663 | solution.py:36
  128.7 0.7 dynamic_slice.54
  130.1 0.7 fusion.52
  132.0 0.7 dynamic_slice.54
  133.4 0.7 fusion.52
  135.4 1.5 collective-permute-start.2
  137.0 8.5 %while.22 = (s32[]{:T(128)}, bf16[2,512,128]{2,1,0:T(8,128)(2,1)S(1)}, s32[2]{0:T(128)S(1)}, s32[1024]{0:T(1024)S(1)}, s32[8,1,128]{2,1,0:T(1,128)S(1)}, /*index...) while((s32[]{:T(128)}, ...), condition=%wide.region_3.4_spmd.clone, body=%wide.region_0.3_spmd.clone.sunk | while | flops 274267648 | bytes 8151267 | solution.py:36
  137.0 0.6 dynamic_slice.51
  138.3 1.8 fusion.47
  141.2 0.6 dynamic_slice.51
  142.6 1.8 fusion.47
  145.5 0.9 slice.43
  146.5 14.4 %collective-permute-done.2 = bf16[2,2,128,1024]{3,2,1,0:T(8,128)(2,1)} collective-permute-done((bf16[2,2,128,1024]{3,2,1,0:T(8,128)(2,1)S(1)}, bf16[2,2,128,1024]{3,2,1,0:T(8,128)(2,1)}, u32[]{:S(2)}, u32[]{:S(2)}) %collective-permute-start.2) | collective-permute-done | bytes 1048608 | tf_op jit(solution)/shard_map/ppermute | solution.py:467
  160.9 1.7 broadcast_select_fusion
  162.8 41.8 %shard_map.56 = bf16[128,4096]{1,0:T(8,128)(2,1)S(1)} custom-call(bf16[1024,256]{1,0:T(8,128)(2,1)S(1)} %pad_maximum_fusion.ho, bf16[4,256,128]{2,1,0:T(8,128)(2,1)S(1)} %broadcast_in_dim.45.mask, bf16[512,1024]{1,0:T(8,128)(2,1)S(1)} %bitcast.81, bf16[512,1024]{1,0:T(8,128)(2,1)S(1)} %bitcast.83, bf16[512,1024]{1,0:T(8,128)(2,1)S(1)} %bitcast.79, ...), custom_call_target="tpu_custom_call" | custom-call | flops 4294967296 | bytes 8388608 | tf_op jit(solution)/shard_map/pallas_call | solution.py:432
  204.7 1.0 copy.26
  (43 shorter events, 5.6 us)
Async XLA Ops:
  106.8 28.5 %collective-permute-start = (bf16[2,2,128,1024]{3,2,1,0:T(8,128)(2,1)}, bf16[2,2,128,1024]{3,2,1,0:T(8,128)(2,1)S(1)}, u32[]{:S(2)}, u32[]{:S(2)}) collective-permute-start(bf16[2,2,128,1024]{3,2,1,0:T(8,128)(2,1)} %get-tuple-element.110), channel_id=1, source_target_pairs={{8,16},{12,20},{16,24},{20,28},{9,17},{13,21},{17,25},{21,29},{10,... | collective-permute-start | bytes 3145736 | tf_op jit(solution)/shard_map/ppermute | solution.py:464
  107.5 27.8 %collective-permute-start.1 = (bf16[2,2,128,1024]{3,2,1,0:T(8,128)(2,1)}, bf16[2,2,128,1024]{3,2,1,0:T(8,128)(2,1)S(1)}, u32[]{:S(2)}, u32[]{:S(2)}) collective-permute-start(bf16[2,2,128,1024]{3,2,1,0:T(8,128)(2,1)} %get-tuple-element.109), channel_id=1, source_target_pairs={{8,0},{12,4},{16,8},{20,12},{9,1},{13,5},{17,9},{21,13},{10,2},{14... | collective-permute-start | bytes 3145736 | tf_op jit(solution)/shard_map/ppermute | solution.py:465
  109.7 11.1 %copy-start.3 = (bf16[2,2,4096,384]{3,2,1,0:T(8,128)(2,1)S(1)}, bf16[2,2,4096,384]{3,2,1,0:T(8,128)(2,1)}, u32[]{:S(2)}) copy-start(bf16[2,2,4096,384]{3,2,1,0:T(8,128)(2,1)} %get-tuple-element.106) | copy-start | bytes 37748740
  109.7 11.2 %copy-start.4 = (bf16[1024,4096]{1,0:T(8,128)(2,1)S(1)}, bf16[1024,4096]{1,0:T(8,128)(2,1)}, u32[]{:S(2)}) copy-start(bf16[1024,4096]{1,0:T(8,128)(2,1)} %get-tuple-element.105) | copy-start | bytes 25165828
  135.4 25.5 %collective-permute-start.2 = (bf16[2,2,128,1024]{3,2,1,0:T(8,128)(2,1)S(1)}, bf16[2,2,128,1024]{3,2,1,0:T(8,128)(2,1)}, u32[]{:S(2)}, u32[]{:S(2)}) collective-permute-start(bf16[2,2,128,1024]{3,2,1,0:T(8,128)(2,1)S(1)} %broadcast_select_fusion.1), channel_id=1, source_target_pairs={{8,0},{12,4},{16,24},{20,28},{9,1},{13,5},{17,25},{21,29},{10,2},{... | collective-permute-start | bytes 3145736 | tf_op jit(solution)/shard_map/ppermute | solution.py:467
  137.0 23.9 %copy-start.1 = (bf16[2,2,128,1024]{3,2,1,0:T(8,128)(2,1)S(1)}, bf16[2,2,128,1024]{3,2,1,0:T(8,128)(2,1)}, u32[]{:S(2)}) copy-start(bf16[2,2,128,1024]{3,2,1,0:T(8,128)(2,1)} %get-tuple-element.110) | copy-start | bytes 3145732
  138.3 2.3 %copy-start.2 = (bf16[1024,128]{1,0:T(8,128)(2,1)S(1)}, bf16[1024,128]{1,0:T(8,128)(2,1)}, u32[]{:S(2)}) copy-start(bf16[1024,128]{1,0:T(8,128)(2,1)} %get-tuple-element.380) | copy-start | bytes 786436 | tf_op jit(solution)/shard_map/while
  142.6 2.3 %copy-start.2 = (bf16[1024,128]{1,0:T(8,128)(2,1)S(1)}, bf16[1024,128]{1,0:T(8,128)(2,1)}, u32[]{:S(2)}) copy-start(bf16[1024,128]{1,0:T(8,128)(2,1)} %get-tuple-element.380) | copy-start | bytes 786436 | tf_op jit(solution)/shard_map/while
  146.5 16.3 %copy-start = (bf16[2,2,128,1024]{3,2,1,0:T(8,128)(2,1)S(1)}, bf16[2,2,128,1024]{3,2,1,0:T(8,128)(2,1)}, u32[]{:S(2)}) copy-start(bf16[2,2,128,1024]{3,2,1,0:T(8,128)(2,1)} %w_out.1) | copy-start | bytes 3145732

commit v4 on v3

--- a/solution.py
+++ b/solution.py
@@ -362,11 +362,12 @@
                 lhs[g, :, h * 128:(h + 1) * 128] = part - image
                 lhs[g, :, width + h * 128:width + (h + 1) * 128] = image
 
-        @pl.loop(0, cols // 256)
-        def _(tile):
-            at = rows_of(tile, 256)
-            for away in range(2):
-                side = (1 - y) if away else y
+        for away in (1, 0):
+            side = (1 - y) if away else y
+
+            @pl.loop(0, cols // 256)
+            def _(tile):
+                at = rows_of(tile, 256)
                 total = None
                 for g in range(4):
                     part = jnp.dot(
@@ -379,6 +380,9 @@
                 else:
                     keep[j, :, at] = total
 
+            if away:
+                y_copies[j].start()
+
     y_copies = [
         remote(sent.at[j], arrived.at[j], y_send.at[j], y_recv.at[j], y_peer) for j in range(4)
     ]
@@ -400,19 +404,15 @@
     for i in range(4):
         g_copy(1, i).wait_recv()
     project(1)
-    y_copies[1].start()
     for i in range(4):
         g_copy(0, i).wait_recv()
         g_copy(2, i).start()
     project(2)
-    y_copies[2].start()
     for i in range(4):
         g_copy(2, i).wait_recv()
     project(3)
-    y_copies[3].start()
     finish(1)
     project(0)
-    y_copies[0].start()
     finish(2)
     finish(3)
     finish(0)

time: 206 us -> 205 us (level)
  no operation moved by 1% of the time
where the time goes in v4:
time: 205 us
  Pallas kernels  147 us (72%)
  matrix products  25.1 us (12%)
  waiting for transfers between devices  14.4 us (7%)
  local copies, waits for them, and re-layouts  7.12 us (3%)
  other arithmetic  5.34 us (3%)
  starting transfers between devices  3.49 us (2%)
  loops' own time  2.74 us (1%)
    pallas_call x1, Pallas kernels, gather_all(): pl.pallas_call(gather_kernel, out_shape=(jax.ShapeDtypeStruct((tok.shape[...  105 us
    pallas_call x1, Pallas kernels, out_project(): pl.pallas_call(out_kernel, out_shape=jax.ShapeDtypeStruct((rows // 2, col...  41.1 us
    dot_general x2, matrix products, qkv_product(): jnp.einsum('rd,hde->rhe', row_block, weight, preferred_element_type=jnp.f...  17.7 us
    ppermute x1, waiting for transfers between devices, fast_local(): last = lax.ppermute(far, 'seq', end_pairs)  14.4 us
    dot_general x4, matrix products, key_scores(): lax.dot_general(q_block, keys_tile, (((1,), (1,)), ((), ())), preferred_e...  5.02 us
  transfers between devices with their start and end apart: 3, of which 1 were waited for; matrix products, arithmetic and copies ran while one was open for 16% of the time, Pallas kernels for 0%

profile of v4, /device:TPU:0, one launch (start us, length us, event | category | flops | bytes accessed | tf_op | source)
XLA Modules:
  0.0 204.9 jit_solution(8015229187161395348)
XLA Ops:
  0.1 1.3 add_add_fusion.meta
  1.4 105.4 %shard_map.55 = (bf16[1024,4096]{1,0:T(8,128)(2,1)}, s32[4,8,8,128]{3,2,1,0:T(8,128)}, bf16[2,2,4096,384]{3,2,1,0:T(8,128)(2,1)}, bf16[2,2,128,1024]{3,2,1,0:T(8,128)(2,1)}, bf16[2,2,128,1024]{3,2,1,0:T(8,128)(2,1)}) custom-call(bf16[128,4096]{1,0:T(8,128)(2,1)} %bitcast.86, s32[8,128]{1,0:T(8,128)} %add_add_fusion.meta, bf16[2,2,1024,384]{3,2,1,0:T(8,128)(2,1)} %w.1, ...), custom_call_target="tpu_custom_call" | custom-call | bytes 44040192 | tf_op jit(solution)/shard_map/pallas_call | solution.py:286
  106.8 0.7 collective-permute-start
  107.5 1.3 collective-permute-start.1
  108.9 0.8 dynamic-slice_bitcast_fusion
  109.7 11.0 %fusion.16 = bf16[1024,2,384]{2,0,1:T(8,128)(2,1)S(1)} fusion(bf16[1024,4096]{1,0:T(8,128)(2,1)} %get-tuple-element.105, bf16[2,2,4096,384]{3,2,1,0:T(8,128)(2,1)} %get-tuple-element.106), kind=kOutput, calls=%fused_computation.26 | convolution fusion | flops 6442450944 | bytes 16252928 | tf_op jit(solution)/shard_map/rd,hde->rhe/dot_general | solution.py:41
  120.9 6.7 %select_convert_fusion = bf16[1024,2,384]{2,0,1:T(8,128)(2,1)S(1)} fusion(bf16[1024,2,384]{2,0,1:T(8,128)(2,1)S(1)} %fusion.16, bf16[2,2,4096,384]{3,2,1,0:T(8,128)(2,1)S(1)} %copy-done.3, bf16[1024,4096]{1,0:T(8,128)(2,1)S(1)} %copy-done.4, pred[1024]{0:T(1024)(128)(4,1)S(1)} %bitcast.97), kind=kOutput, calls=%fused_computation.34 | convolution fusion | flops 6443237376 | bytes 17826816 | tf_op jit(solution)/shard_map/rd,hde->rhe/dot_general | solution.py:41
  127.5 1.1 slice_bitcast_fusion.3
  128.6 6.6 %while.23 = (s32[]{:T(128)}, bf16[2,512,128]{2,1,0:T(8,128)(2,1)S(1)}, s32[2]{0:T(128)S(1)}, s32[1024]{0:T(1024)S(1)}, s32[8,1,128]{2,1,0:T(1,128)S(1)}, /*index...) while((s32[]{:T(128)}, ...), condition=%wide.region_7.8_spmd.clone, body=%wide.region_4.7_spmd.clone.sunk | while | flops 274267648 | bytes 7102663 | solution.py:36
  128.7 0.7 dynamic_slice.54
  130.1 0.7 fusion.52
  132.0 0.7 dynamic_slice.54
  133.4 0.7 fusion.52
  135.4 1.5 collective-permute-start.2
  137.0 8.5 %while.22 = (s32[]{:T(128)}, bf16[2,512,128]{2,1,0:T(8,128)(2,1)S(1)}, s32[2]{0:T(128)S(1)}, s32[1024]{0:T(1024)S(1)}, s32[8,1,128]{2,1,0:T(1,128)S(1)}, /*index...) while((s32[]{:T(128)}, ...), condition=%wide.region_3.4_spmd.clone, body=%wide.region_0.3_spmd.clone.sunk | while | flops 274267648 | bytes 8151267 | solution.py:36
  137.0 0.6 dynamic_slice.51
  138.3 1.8 fusion.47
  141.2 0.6 dynamic_slice.51
  142.6 1.8 fusion.47
  145.5 0.9 slice.43
  146.5 14.4 %collective-permute-done.2 = bf16[2,2,128,1024]{3,2,1,0:T(8,128)(2,1)} collective-permute-done((bf16[2,2,128,1024]{3,2,1,0:T(8,128)(2,1)S(1)}, bf16[2,2,128,1024]{3,2,1,0:T(8,128)(2,1)}, u32[]{:S(2)}, u32[]{:S(2)}) %collective-permute-start.2) | collective-permute-done | bytes 1048608 | tf_op jit(solution)/shard_map/ppermute | solution.py:467
  160.9 1.7 broadcast_select_fusion
  162.8 41.1 %shard_map.56 = bf16[128,4096]{1,0:T(8,128)(2,1)S(1)} custom-call(bf16[1024,256]{1,0:T(8,128)(2,1)S(1)} %pad_maximum_fusion.ho, bf16[4,256,128]{2,1,0:T(8,128)(2,1)S(1)} %broadcast_in_dim.45.mask, bf16[512,1024]{1,0:T(8,128)(2,1)S(1)} %bitcast.81, bf16[512,1024]{1,0:T(8,128)(2,1)S(1)} %bitcast.83, bf16[512,1024]{1,0:T(8,128)(2,1)S(1)} %bitcast.79, ...), custom_call_target="tpu_custom_call" | custom-call | flops 4294967296 | bytes 8388608 | tf_op jit(solution)/shard_map/pallas_call | solution.py:432
  204.0 1.0 copy.26
  (43 shorter events, 5.6 us)
Async XLA Ops:
  106.8 28.5 %collective-permute-start = (bf16[2,2,128,1024]{3,2,1,0:T(8,128)(2,1)}, bf16[2,2,128,1024]{3,2,1,0:T(8,128)(2,1)S(1)}, u32[]{:S(2)}, u32[]{:S(2)}) collective-permute-start(bf16[2,2,128,1024]{3,2,1,0:T(8,128)(2,1)} %get-tuple-element.110), channel_id=1, source_target_pairs={{8,16},{12,20},{16,24},{20,28},{9,17},{13,21},{17,25},{21,29},{10,... | collective-permute-start | bytes 3145736 | tf_op jit(solution)/shard_map/ppermute | solution.py:464
  107.5 27.8 %collective-permute-start.1 = (bf16[2,2,128,1024]{3,2,1,0:T(8,128)(2,1)}, bf16[2,2,128,1024]{3,2,1,0:T(8,128)(2,1)S(1)}, u32[]{:S(2)}, u32[]{:S(2)}) collective-permute-start(bf16[2,2,128,1024]{3,2,1,0:T(8,128)(2,1)} %get-tuple-element.109), channel_id=1, source_target_pairs={{8,0},{12,4},{16,8},{20,12},{9,1},{13,5},{17,9},{21,13},{10,2},{14... | collective-permute-start | bytes 3145736 | tf_op jit(solution)/shard_map/ppermute | solution.py:465
  109.7 11.1 %copy-start.3 = (bf16[2,2,4096,384]{3,2,1,0:T(8,128)(2,1)S(1)}, bf16[2,2,4096,384]{3,2,1,0:T(8,128)(2,1)}, u32[]{:S(2)}) copy-start(bf16[2,2,4096,384]{3,2,1,0:T(8,128)(2,1)} %get-tuple-element.106) | copy-start | bytes 37748740
  109.7 11.2 %copy-start.4 = (bf16[1024,4096]{1,0:T(8,128)(2,1)S(1)}, bf16[1024,4096]{1,0:T(8,128)(2,1)}, u32[]{:S(2)}) copy-start(bf16[1024,4096]{1,0:T(8,128)(2,1)} %get-tuple-element.105) | copy-start | bytes 25165828
  135.4 25.5 %collective-permute-start.2 = (bf16[2,2,128,1024]{3,2,1,0:T(8,128)(2,1)S(1)}, bf16[2,2,128,1024]{3,2,1,0:T(8,128)(2,1)}, u32[]{:S(2)}, u32[]{:S(2)}) collective-permute-start(bf16[2,2,128,1024]{3,2,1,0:T(8,128)(2,1)S(1)} %broadcast_select_fusion.1), channel_id=1, source_target_pairs={{8,0},{12,4},{16,24},{20,28},{9,1},{13,5},{17,25},{21,29},{10,2},{... | collective-permute-start | bytes 3145736 | tf_op jit(solution)/shard_map/ppermute | solution.py:467
  137.0 23.9 %copy-start.1 = (bf16[2,2,128,1024]{3,2,1,0:T(8,128)(2,1)S(1)}, bf16[2,2,128,1024]{3,2,1,0:T(8,128)(2,1)}, u32[]{:S(2)}) copy-start(bf16[2,2,128,1024]{3,2,1,0:T(8,128)(2,1)} %get-tuple-element.110) | copy-start | bytes 3145732
  138.3 2.3 %copy-start.2 = (bf16[1024,128]{1,0:T(8,128)(2,1)S(1)}, bf16[1024,128]{1,0:T(8,128)(2,1)}, u32[]{:S(2)}) copy-start(bf16[1024,128]{1,0:T(8,128)(2,1)} %get-tuple-element.380) | copy-start | bytes 786436 | tf_op jit(solution)/shard_map/while
  142.6 2.3 %copy-start.2 = (bf16[1024,128]{1,0:T(8,128)(2,1)S(1)}, bf16[1024,128]{1,0:T(8,128)(2,1)}, u32[]{:S(2)}) copy-start(bf16[1024,128]{1,0:T(8,128)(2,1)} %get-tuple-element.380) | copy-start | bytes 786436 | tf_op jit(solution)/shard_map/while
  146.5 16.3 %copy-start = (bf16[2,2,128,1024]{3,2,1,0:T(8,128)(2,1)S(1)}, bf16[2,2,128,1024]{3,2,1,0:T(8,128)(2,1)}, u32[]{:S(2)}) copy-start(bf16[2,2,128,1024]{3,2,1,0:T(8,128)(2,1)} %w_out.1) | copy-start | bytes 3145732
